TPU v7x, 768 devices: a whole 4x8x12 slice. The times are simulated.
768 devices in a mesh: row: 16 (over z_lo, x), col: 48 (over z_hi, y, core).
Axes of the slice: x: 4, y: 8, z: 12 (z_hi: 3, z_lo: 4; z = z_hi * 4 + z_lo), core: 2. Of those that a mesh axis runs over, the one named last changes fastest.
Arguments:
- stored: float32 [4096, 12288], P('row', 'col'), may hold values from -6 to 6
- destination: int32 [4096], P('row'), may hold values from 0 to 4095, as said below
- tile_mask: int32 [16, 48], replicated, may hold values from 0 to 1, as said below
- integrals: bfloat16 [12288, 12288], P('row', 'col'), may hold values from -0.0546875 to 0.0546875
- denominators: float32 [4096, 12288], P('row', 'col'), may hold values from 0.5 to 4
Outputs:
- residual: float32 [4096, 12288], P('row', 'col')
Inputs may be any that keep to these rules, and one draw needn't show every extreme that they name: destination is a permutation of the 4096 occupied pairs; the rows of each aligned block of 256 stored rows name exactly 16 occupied pairs in each aligned block of 256 occupied pairs. In every row of tile_mask, tile columns t and t + 1, for every even t, hold one 1 and one 0; so each row holds exactly 24 ones.
All inputs are finite; a program needn't handle non-finite values.
Results may differ from a plain program's by a relative error of at most 0.0029.
Values may be sent and summed in bfloat16 or wider, within the bound.
A program may use at most 32 MiB of HBM per device.

v0:
```python
import jax
import jax.numpy as jnp
from jax import lax
from jax.sharding import PartitionSpec as P

TILE = 256


def mask_block(tile_mask, row_first, row_count, col_first, col_count):
    row_tiles = (row_first + jnp.arange(row_count, dtype=jnp.int32)) // TILE
    col_tiles = (col_first + jnp.arange(col_count, dtype=jnp.int32)) // TILE
    row_pick = (
        row_tiles[:, None] == jnp.arange(tile_mask.shape[0], dtype=jnp.int32)[None, :]
    ).astype(jnp.float32)
    col_pick = (
        col_tiles[:, None] == jnp.arange(tile_mask.shape[1], dtype=jnp.int32)[None, :]
    ).astype(jnp.float32)
    row_mask = jnp.dot(row_pick, tile_mask.astype(jnp.float32), preferred_element_type=jnp.float32)
    return jnp.dot(row_mask, col_pick.T, preferred_element_type=jnp.float32)


def local(stored, destination, tile_mask, integrals, denominators):
    row_count, col_width = stored.shape
    row_index = lax.axis_index("row")
    col_index = lax.axis_index("col")
    group_count = lax.axis_size("row")
    per_group = row_count // group_count
    target_block = destination // row_count
    ordering = jnp.argsort(target_block, stable=True)
    outgoing = stored[ordering].reshape(group_count, per_group, col_width)
    out_dest = destination[ordering].reshape(group_count, per_group)
    incoming, in_dest = (
        lax.all_to_all(
            outgoing.astype(jnp.bfloat16), "row", split_axis=0, concat_axis=0, tiled=True
        ).astype(outgoing.dtype),
        lax.all_to_all(out_dest, "row", split_axis=0, concat_axis=0, tiled=True),
    )
    local_slot = in_dest.reshape(row_count) - row_index * row_count
    placed = (
        jnp.zeros((row_count, col_width), jnp.float32)
        .at[local_slot]
        .set(incoming.reshape(row_count, col_width))
    )
    kept_mask = mask_block(
        tile_mask, row_index * row_count, row_count, col_index * col_width, col_width
    )
    amplitudes = jnp.where(kept_mask > 0.5, placed, 0.0).astype(jnp.bfloat16)
    amp_strip = lax.all_gather(amplitudes, "col", axis=1, tiled=True)
    ladder = jnp.dot(
        amp_strip,
        lax.all_gather(integrals, "row", axis=0, tiled=True),
        preferred_element_type=jnp.float32,
    )
    return ladder / denominators


def solution(mesh):
    return jax.shard_map(
        local,
        mesh=mesh,
        in_specs=(P("row", "col"), P("row"), P(), P("row", "col"), P("row", "col")),
        out_specs=P("row", "col"),
        check_vma=False,
    )
```

profile of v0, /device:TPU:1, one launch (start us, length us, event | category | flops | bytes accessed | tf_op | source)
XLA Modules:
  0.0 270.7 jit_solution(6967605423911632709)
XLA Ops:
  6.5 0.0 copy-start
  6.5 0.0 all-gather.5.cloned.1.call-start
  6.5 0.7 all-gather.5.cloned.1.call-update
  7.3 0.7 and_select_fusion
  8.0 3.2 %sort.17 = (s32[256]{0:T(256)}, s32[256]{0:T(256)S(1)}) sort(s32[256]{0:T(256)S(1)} %and_select_fusion, s32[256]{0:T(256)S(1)} %iota.24), dimensions={0}, to_apply=%region_0.1 | sort | flops 2048 | bytes 4096 | tf_op jit(solution)/shard_map/jit(argsort)/sort | solution.py:29
  11.1 2.0 gather_fusion
  13.1 0.7 all_to_all.9
  13.8 10.4 %all-to-all-start = ((s32[16,1,16]{2,1,0:T(1,128)}), s32[16,1,16]{2,1,0:T(1,128)S(1)}, u32[]{:S(2)}, u32[]{:S(2)}) async-start(s32[16,1,16]{2,1,0:T(1,128)} %all_to_all.9), calls=%async_computation | async-start | bytes 16384 | tf_op jit(solution)/shard_map/all_to_all | solution.py:36
  24.2 0.0 copy-done
  24.2 1.6 gather_fusion.1
  25.8 5.1 %all-to-all-done = s32[16,1,16]{2,1,0:T(1,128)S(1)} async-done(((s32[16,1,16]{2,1,0:T(1,128)}), s32[16,1,16]{2,1,0:T(1,128)S(1)}, u32[]{:S(2)}, u32[]{:S(2)}) %all-to-all-start) | async-done | bytes 1056 | tf_op jit(solution)/shard_map/all_to_all | solution.py:36
  30.9 3.5 %all-to-all-start.1 = ((bf16[16,16,256]{2,1,0:T(8,128)(2,1)}), bf16[16,16,256]{2,1,0:T(8,128)(2,1)S(1)}, u32[]{:S(2)}, u32[]{:S(2)}) async-start(bf16[16,16,256]{2,1,0:T(8,128)(2,1)} %bitcast.1), calls=%async_computation.1 | async-start | bytes 262144 | tf_op jit(solution)/shard_map/all_to_all | solution.py:33
  34.5 0.0 all-gather.3.cloned.1.call-start
  34.6 0.1 sub.32
  34.7 7.9 %all-to-all-done.1 = bf16[16,16,256]{2,1,0:T(8,128)(2,1)S(1)} async-done(((bf16[16,16,256]{2,1,0:T(8,128)(2,1)}), bf16[16,16,256]{2,1,0:T(8,128)(2,1)S(1)}, u32[]{:S(2)}, u32[]{:S(2)}) %all-to-all-start.1) | async-done | bytes 131104 | tf_op jit(solution)/shard_map/all_to_all | solution.py:33
  42.6 1.5 scatter_custom_fusion
  44.1 1.7 fusion.1
  45.8 0.0 all-gather.3.cloned.1.call-update
  45.8 64.5 %all-gather.5.cloned.1.call-done = bf16[12288,256]{1,0:T(8,128)(2,1)} async-done(((bf16[768,256]{1,0:T(8,128)(2,1)}), bf16[12288,256]{1,0:T(8,128)(2,1)}) %all-gather.5.cloned.1.call-update) | async-done | bytes 6291472 | tf_op jit(solution)/shard_map/all_gather | solution.py:51
  110.3 146.5 %all-gather.3.cloned.1.call-done = bf16[256,12288]{1,0:T(8,128)(2,1)} async-done(((bf16[256,256]{1,0:T(8,128)(2,1)}), bf16[256,12288]{1,0:T(8,128)(2,1)}) %all-gather.3.cloned.1.call-update) | async-done | bytes 6291472 | tf_op jit(solution)/shard_map/all_gather | solution.py:48
  256.8 7.1 %convolution_divide_fusion = f32[256,256]{1,0:T(8,128)} fusion(f32[256,256]{1,0:T(8,128)} %param.9, bf16[256,12288]{1,0:T(8,128)(2,1)} %all-gather.3.cloned.1.call-done, bf16[12288,256]{1,0:T(8,128)(2,1)} %all-gather.5.cloned.1.call-done), kind=kOutput, calls=%fused_computation.6 | convolution fusion | flops 1610678272 | bytes 13107200 | tf_op jit(solution)/shard_map/dot_general | solution.py:49
  (6 shorter events, 0.1 us)
Async XLA Ops:
  6.5 17.7 %copy-start = (f32[256,256]{1,0:T(8,128)S(1)}, f32[256,256]{1,0:T(8,128)}, u32[]{:S(2)}) copy-start(f32[256,256]{1,0:T(8,128)} %param.5) | copy-start | bytes 786436
  6.5 103.8 %all-gather.5.cloned.1.call-start = ((), (), s32[]{:S(2)}) async-start(), calls=%async_computation.3 | async-start | bytes 6684672 | tf_op jit(solution)/shard_map/all_gather | solution.py:51
  13.8 17.1 %all-to-all-start = ((s32[16,1,16]{2,1,0:T(1,128)}), s32[16,1,16]{2,1,0:T(1,128)S(1)}, u32[]{:S(2)}, u32[]{:S(2)}) async-start(s32[16,1,16]{2,1,0:T(1,128)} %all_to_all.9), calls=%async_computation | async-start | bytes 16384 | tf_op jit(solution)/shard_map/all_to_all | solution.py:36
  30.9 11.6 %all-to-all-start.1 = ((bf16[16,16,256]{2,1,0:T(8,128)(2,1)}), bf16[16,16,256]{2,1,0:T(8,128)(2,1)S(1)}, u32[]{:S(2)}, u32[]{:S(2)}) async-start(bf16[16,16,256]{2,1,0:T(8,128)(2,1)} %bitcast.1), calls=%async_computation.1 | async-start | bytes 262144 | tf_op jit(solution)/shard_map/all_to_all | solution.py:33
  34.5 222.3 %all-gather.3.cloned.1.call-start = ((), (), s32[]{:S(2)}) async-start(), calls=%async_computation.2 | async-start | bytes 6422528 | tf_op jit(solution)/shard_map/all_gather | solution.py:48
Sparse Core Ops, SparseCore 0:
  9.7 100.5 all-gather.4
  114.2 142.5 all-gather.2
where the time goes:
time: 271 us
  waiting for transfers between devices  225 us (83%)
  starting transfers between devices  13.9 us (5%)
  between operations  13.5 us (5%)
  matrix products  8.81 us (3%)
  other arithmetic  5.42 us (2%)
  local copies, waits for them, and re-layouts  4.39 us (2%)
    all_gather x1, waiting for transfers between devices, local(): amp_strip = lax.all_gather(amplitudes, 'col', axis=1, tiled=True)  147 us
    all_gather x1, waiting for transfers between devices, local(): lax.all_gather(integrals, 'row', axis=0, tiled=True)  64.5 us
    all_to_all x1, starting transfers between devices, local(): lax.all_to_all(out_dest, 'row', split_axis=0, concat_axis=0, tiled=True)  10.4 us
    all_to_all x1, waiting for transfers between devices, local(): lax.all_to_all(outgoing.astype(jnp.bfloat16), 'row', split_axis=0, concat...  7.93 us
    dot_general x1, matrix products, local(): jnp.dot(amp_strip, lax.all_gather(integrals, 'row', axis=0, tiled=True),...  7.09 us
  transfers between devices with their start and end apart: 4, of which 4 were waited for; matrix products, arithmetic and copies ran while one was open for 4% of the time, Pallas kernels for 0%

commit v1 on v0

v1 whole, which is shorter than its diff:
```python
import jax
import jax.numpy as jnp
from jax import lax
from jax.experimental import pallas as pl
from jax.experimental.pallas import tpu as pltpu
from jax.sharding import PartitionSpec as P

MESH = pl.DeviceIdType.MESH
BF, F32, I32 = jnp.bfloat16, jnp.float32, jnp.int32
NX, NY, NZL, NZH = 4, 8, 4, 3
T = 256
KB = 768
HB = KB // 2
NP = 6
ORDER = [
    (0, 0), (1, 0), (0, 1), (1, 1), (2, 0), (0, 2), (1, 2), (2, 1), (3, 0), (0, 3), (1, 3), (2, 2), (3, 1),
    (0, 4), "B", (0, None), (1, 4), (2, 3), (3, 2), (1, None), (2, 4), (3, 3), (2, None), (3, 4), (3, None),
]


def iota(shape, dim):
    return lax.broadcasted_iota(I32, shape, dim)


def kernel(
    stored, dest, mask, b_hbm, den, out,
    t_ref, sib, merged, a_ref, b_ref, c_tx, c_rx, slots, w_ref,
    sib_s, a1_s, a_s, a_r, b_s, b_r, bs_s, bs_r, bl_s, c_s, c_r, q_s, q_r,
):
    r, c = lax.axis_index("row"), lax.axis_index("col")
    zl, x = r // 4, r % 4
    zh, y, k = c // 16, (c // 2) % 8, c % 2

    def dev(x_, y_, zl_, zh_, k_):
        return (zl_ * 4 + x_, zh_ * 16 + y_ * 2 + k_)

    sibling = (r, c + 1 - 2 * k)
    xr, xl = dev((x + 1) % 4, y, zl, zh, k), dev((x + 3) % 4, y, zl, zh, k)
    yr, yl = dev(x, (y + 1) % 8, zl, zh, k), dev(x, (y + 7) % 8, zl, zh, k)

    def remote(src, dst, s, rr, d):
        return pltpu.make_async_remote_copy(
            src_ref=src, dst_ref=dst, send_sem=s, recv_sem=rr, device_id=d, device_id_type=MESH
        )

    def arrived(ref, sem):
        pltpu.make_async_copy(ref, ref, sem).wait()

    bar = pltpu.get_barrier_semaphore()

    def hello(d):
        pl.semaphore_signal(bar, inc=1, device_id=d, device_id_type=MESH)

    @pl.loop(0, 8)
    def _(i):
        hello(dev(x, y, i % 4, (zh + 1 + i // 4) % 3, k))

    me = r * 2 + k

    @pl.loop(1, 32)
    def _(i):
        o = (me + i) % 32
        hello((o // 2, c - k + o % 2))

    hello(yr)
    hello(yl)

    own_b = pltpu.make_async_copy(b_hbm, b_ref.at[k, pl.ds(x * KB, KB)], bl_s)
    own_b.start()
    d = dest[...]
    blk = lax.shift_right_logical(d, 8)
    low = jnp.bitwise_and(d, 255)
    oh = (iota((16, T), 0) == blk).astype(F32)
    before = (iota((T, T), 0) < iota((T, T), 1)).astype(F32).astype(BF)
    cum = jnp.dot(oh.astype(BF), before, preferred_element_type=F32)
    rank = jnp.sum(oh * cum, axis=0, keepdims=True)
    pos = blk * 16 + rank.astype(I32)
    perm = iota((T, T), 0) == pos
    tm = mask[...].astype(F32).astype(BF)
    spread = (lax.shift_right_logical(iota((T, 16), 0), 4) == iota((T, 16), 1)).astype(F32).astype(BF)
    wide = jnp.dot(spread, tm, preferred_element_type=F32)
    keep = jnp.sum(jnp.where(iota(wide.shape, 1) == c, wide, 0.0), axis=1, keepdims=True)
    permf = perm.astype(F32)
    t_ref[...] = jnp.dot((permf * keep).astype(BF), stored[...].astype(BF), preferred_element_type=F32).astype(BF)
    low8 = jnp.broadcast_to(low, (8, T)).astype(F32).astype(BF)
    srow = lax.dot_general(low8, permf.astype(BF), (((1,), (1,)), ((), ())), preferred_element_type=F32)
    slots[r] = srow[:1]
    half = (k * 8 + lax.shift_right_logical(iota((128, 16), 0), 4) == iota((128, 16), 1)).astype(F32).astype(BF)
    pick = (iota((48, 128), 0) == 12 * zl + iota((48, 128), 1)).astype(F32).astype(BF)
    tiles = jnp.dot(half, tm, preferred_element_type=F32).astype(BF)
    w_ref[...] = jnp.dot(tiles, pick, preferred_element_type=F32)

    pl.semaphore_wait(bar, 41)

    away, mine = pl.ds((1 - k) * 128, 128), pl.ds(k * 128, 128)
    to_sib = remote(t_ref.at[away], sib, sib_s.at[0], sib_s.at[1], sibling)
    to_sib.start()
    top, bot = pl.ds(0, HB), pl.ds(HB, HB)

    def bslot(n, xx, h):
        return b_ref.at[n, pl.ds(xx * KB + h * HB, HB)]

    b_out = [
        remote(b_hbm.at[top], bslot(k, x, 0), b_s.at[0], b_r.at[x, 0], xr),
        remote(b_hbm.at[bot], bslot(k, x, 1), b_s.at[1], b_r.at[x, 1], xl),
        remote(b_hbm.at[bot], bslot(k, x, 1), b_s.at[2], b_r.at[x, 1], xr),
        remote(b_hbm.at[top], bslot(k, x, 0), b_s.at[3], b_r.at[x, 0], xl),
    ]
    for cp in b_out:
        cp.start()
    to_sib.wait_recv()
    merged[...] = t_ref[mine] + sib[...]

    j = zh * 8 + y
    tzl, tp = j // 6, j % 6
    a1 = []
    for h in range(NZH):
        self_ = jnp.logical_and(tzl == zl, zh == h)
        cp = remote(merged, a_ref.at[zl, tp], a1_s.at[h], a_r.at[zl, tp], dev(x, y, tzl, h, k))
        a1.append((jnp.logical_not(self_), cp))

        @pl.when(jnp.logical_not(self_))
        def _():
            cp.start()

        @pl.when(self_)
        def _():
            pltpu.make_async_copy(merged, a_ref.at[zl, tp], a_r.at[zl, tp]).start()

    def slot_cp(i):
        o = (r + i) % 16
        return remote(slots.at[r], slots.at[r], q_s, q_r, (o, c))

    @pl.loop(1, 16)
    def _(i):
        slot_cp(i).start()

    xa, xb, xc = (x + 3) % 4, (x + 1) % 4, (x + 2) % 4
    b_sib = []

    def to_sibling(src, xx, h):
        cp = remote(src, bslot(k, xx, h), bs_s.at[len(b_sib)], bs_r.at[xx, h], sibling)
        cp.start()
        b_sib.append(cp)

    arrived(bslot(k, xa, 0), b_r.at[xa, 0])
    relay0 = remote(bslot(k, xa, 0), bslot(k, xa, 0), b_s.at[4], b_r.at[xa, 0], xr)
    relay0.start()
    arrived(bslot(k, xb, 1), b_r.at[xb, 1])
    relay1 = remote(bslot(k, xb, 1), bslot(k, xb, 1), b_s.at[5], b_r.at[xb, 1], xl)
    relay1.start()
    b_out += [relay0, relay1]
    to_sibling(b_hbm.at[top], x, 0)
    to_sibling(b_hbm.at[bot], x, 1)
    to_sibling(bslot(k, xa, 0), xa, 0)
    to_sibling(bslot(k, xb, 1), xb, 1)

    u = (y + 2 * zl) % 8

    def a_cp(q, p, way):
        return remote(a_ref.at[q, p], a_ref.at[q, p], a_s.at[q, p, way], a_r.at[q, p], (yr, yl)[way])

    def reach(p, way):
        far = jnp.where(p >= 3, 1, 0)
        return 3 + far if way == 0 else 4 - far

    def ring(q, s, waits=False):
        for way in ((0, 1) if s else (0,)):
            p = (u - s + 8 * way + 8 - 8 * way) % 8 if way == 0 else (u + s) % 8
            valid = p < NP
            if s:
                valid = jnp.logical_and(valid, s <= reach(p, way))

            @pl.when(valid)
            def _():
                if not waits:
                    arrived(a_ref.at[q, p], a_r.at[q, p])
                for w in ((way,) if s else (0, 1)):
                    if s >= 4:
                        continue

                    @pl.when(s < reach(p, w))
                    def _():
                        if waits:
                            a_cp(q, p, w).wait_send()
                        else:
                            a_cp(q, p, w).start()

    def c_send(q, i, act):
        o, n = k * 8 + i % 8, i // 8
        src = c_tx.at[q * 16 + i]
        dst = c_rx.at[zl, q * 4 + x]
        self_ = jnp.logical_and(o == r, n == k)

        @pl.when(jnp.logical_not(self_))
        def _():
            remote(src, dst, c_s, c_r, (o, c - k + n)).start()

        @pl.when(self_)
        def _():
            pltpu.make_async_copy(src, dst, c_r).start()

    def product(q):
        w = w_ref[...]
        for n in range(2):
            acc = jnp.zeros((128, T), F32)
            for p in range(NP):
                a = a_ref[q, p]
                for e in range(2):
                    keep_ = w[:, 2 * p + e : 2 * p + e + 1] > 0.5
                    lhs = jnp.where(keep_, a.astype(F32), 0.0).astype(BF)
                    acc = acc + jnp.dot(lhs, b_ref[n, (2 * p + e) * T : (2 * p + e + 1) * T], preferred_element_type=F32)
            c_tx[q * 16 + n * 8 : q * 16 + n * 8 + 8] = acc.astype(BF).reshape(8, 16, T)

        @pl.loop(0, 16)
        def _(i):
            c_send(q, i, None)

    for step in ORDER:
        if step == "B":
            for xx, h in ((xa, 1), (xb, 0), (xc, 0), (xc, 1)):
                arrived(bslot(k, xx, h), b_r.at[xx, h])
                to_sibling(bslot(k, xx, h), xx, h)
            own_b.wait()
            for xx in range(4):
                for h in range(2):
                    arrived(bslot(1 - k, xx, h), bs_r.at[xx, h])
        elif step[1] is None:
            product(step[0])
        else:
            ring(*step)

    to_sib.wait_send()
    for ok, cp in a1:

        @pl.when(ok)
        def _():
            cp.wait_send()

    for cp in b_out + b_sib:
        cp.wait_send()
    for step in ORDER:
        if step != "B" and step[1] is not None and step[1] < 4:
            ring(*step, waits=True)
    arrived(slots.at[pl.ds(0, 15)], q_s)
    arrived(slots.at[pl.ds(0, 15)], q_r)

    sel = (iota((T, T), 0) == r * 16 + jnp.bitwise_and(iota((T, T), 1), 15)).astype(F32).astype(BF)
    g = jnp.dot(slots[...].reshape(16, T).astype(BF), sel, preferred_element_type=F32)
    own = lax.shift_right_logical(iota((16, T), 1), 4) == iota((16, T), 0)
    at = jnp.sum(jnp.where(own, g, 0.0), axis=0, keepdims=True).astype(I32)
    place = (iota((T, T), 0) == at).astype(F32).astype(BF)

    arrived(c_rx, c_r)
    total = jnp.zeros((T, T), F32)
    for g in range(NZL):
        total = total + jnp.dot(place, c_rx[g].reshape(T, T), preferred_element_type=F32)
    out[...] = total / den[...]

    has_own = (r // 8) == k

    @pl.when(has_own)
    def _():
        arrived(c_tx.at[pl.ds(0, 60)], c_s)

    @pl.when(jnp.logical_not(has_own))
    def _():
        arrived(c_tx, c_s)


def local(stored, destination, tile_mask, integrals, denominators):
    vm = pl.BlockSpec(memory_space=pltpu.VMEM)
    dma = pltpu.SemaphoreType.DMA
    return pl.pallas_call(
        kernel,
        out_shape=jax.ShapeDtypeStruct((T, T), F32),
        in_specs=[vm, vm, vm, pl.BlockSpec(memory_space=pl.ANY), vm],
        out_specs=vm,
        scratch_shapes=[
            pltpu.VMEM((T, T), BF),
            pltpu.VMEM((128, T), BF),
            pltpu.VMEM((128, T), BF),
            pltpu.VMEM((4, NP, 128, T), BF),
            pltpu.VMEM((2, 4 * KB, T), BF),
            pltpu.VMEM((64, 16, T), BF),
            pltpu.VMEM((4, 16, 16, T), BF),
            pltpu.VMEM((16, 1, T), F32),
            pltpu.VMEM((128, 128), F32),
            dma((2,)),
            dma((3,)),
            dma((4, NP, 2)),
            dma((4, NP)),
            dma((6,)),
            dma((4, 2)),
            dma((8,)),
            dma((4, 2)),
            dma,
            dma,
            dma,
            dma,
            dma,
        ],
        compiler_params=pltpu.CompilerParams(
            collective_id=0, has_side_effects=True, vmem_limit_bytes=40 << 20
        ),
        name="ladder",
    )(stored, destination.reshape(1, T), tile_mask, integrals, denominators)


def solution(mesh):
    return jax.shard_map(
        local,
        mesh=mesh,
        in_specs=(P("row", "col"), P("row"), P(), P("row", "col"), P("row", "col")),
        out_specs=P("row", "col"),
        check_vma=False,
    )
```

time: 271 us -> 72.5 us (0.27)
  waiting for transfers between devices: 225 us -> 0 us
  Pallas kernels: 0 us -> 67.2 us
  starting transfers between devices: 13.9 us -> 0 us
  between operations: 13.5 us -> 0.01 us
  matrix products: 8.81 us -> 0 us
  other arithmetic: 5.42 us -> 0 us
    all_gather x2 -> x0, waiting for transfers between devices: 211 us -> none  [the longest x1 147 us: local(): amp_strip = lax.all_gather(amplitudes, 'col', axis=1, tiled=True)]
    pallas_call x0 -> x1, Pallas kernels: none -> 67.2 us  [local(): pl.pallas_call(kernel, out_shape=jax.ShapeDtypeStruct((T, T), F32), in_sp...]
    all_to_all x2 -> x0, starting transfers between devices: 13.9 us -> none  [the longest x1 10.4 us: local(): lax.all_to_all(out_dest, 'row', split_axis=0, concat_axis=0, tiled=True)]
    all_to_all x2 -> x0, waiting for transfers between devices: 13 us -> none  [the longest x1 7.93 us: local(): lax.all_to_all(outgoing.astype(jnp.bfloat16), 'row', split_axis=0, concat...]
    dot_general x2 -> x0, matrix products: 8.81 us -> none  [the longest x1 7.09 us: local(): jnp.dot(amp_strip, lax.all_gather(integrals, 'row', axis=0, tiled=True),...]
    unnamed x2 -> x11, local copies, waits for them, and re-layouts: 0.01 us -> 4.97 us
    gather x2 -> x0, local copies, waits for them, and re-layouts: 3.61 us -> none  [the longest x1 1.98 us: local(): out_dest = destination[ordering].reshape(group_count, per_group)]
    sort x1 -> x0, other arithmetic: 3.17 us -> none  [local(): ordering = jnp.argsort(target_block, stable=True)]
  transfers between devices with their start and end apart: 4 -> 0, of which waited for: 4 -> 0; matrix products, arithmetic and copies ran while one was open for 4% -> 0% of each run, Pallas kernels for 0% -> 0%
where the time goes in v1:
time: 72.5 us; the launch traced here: 72.2 us
  Pallas kernels  67.2 us (93%)
  local copies, waits for them, and re-layouts  4.97 us (7%)
    pallas_call x1, Pallas kernels, local(): pl.pallas_call(kernel, out_shape=jax.ShapeDtypeStruct((T, T), F32), in_sp...  67.2 us
    unnamed x11, local copies, waits for them, and re-layouts  4.97 us

profile of v1, /device:TPU:1, one launch (start us, length us, event | category | flops | bytes accessed | tf_op | source)
XLA Modules:
  0.0 72.2 jit_solution(12590858617838463818)
XLA Ops:
  0.0 0.0 copy-start.4
  0.0 0.7 copy-done.4
  0.7 0.0 copy-start
  0.7 1.0 %copy-done = bf16[768,256]{1,0:T(8,128)(2,1)S(1)} copy-done((bf16[768,256]{1,0:T(8,128)(2,1)S(1)}, bf16[768,256]{1,0:T(8,128)(2,1)}, u32[]{:S(2)}) %copy-start) | copy-done | bytes 393240
  1.7 0.0 copy-start.1
  1.7 0.9 %copy-done.1 = f32[256,256]{1,0:T(8,128)S(1)} copy-done((f32[256,256]{1,0:T(8,128)S(1)}, f32[256,256]{1,0:T(8,128)}, u32[]{:S(2)}) %copy-start.1) | copy-done | bytes 262168
  2.6 0.0 copy-start.2
  2.6 0.9 %copy-done.2 = f32[256,256]{1,0:T(8,128)S(1)} copy-done((f32[256,256]{1,0:T(8,128)S(1)}, f32[256,256]{1,0:T(8,128)}, u32[]{:S(2)}) %copy-start.2) | copy-done | bytes 262168
  3.6 0.0 copy-start.3
  3.6 0.7 copy-done.3
  4.3 67.2 %ladder.1 = f32[256,256]{1,0:T(8,128)S(1)} custom-call(f32[256,256]{1,0:T(8,128)S(1)} %copy-done.1, s32[1,256]{1,0:T(1,128)S(1)} %bitcast.1, s32[16,48]{1,0:T(8,128)S(1)} %copy-done.3, bf16[768,256]{1,0:T(8,128)(2,1)S(1)} %copy-done, f32[256,256]{1,0:T(8,128)S(1)} %copy-done.2), custom_call_target="tpu_custom_call" | custom-call | tf_op jit(solution)/shard_map/ladder/pallas_call | solution.py:274
  71.5 0.7 copy.7
Async XLA Ops:
  0.0 0.7 copy-start.4
  0.7 1.0 %copy-start = (bf16[768,256]{1,0:T(8,128)(2,1)S(1)}, bf16[768,256]{1,0:T(8,128)(2,1)}, u32[]{:S(2)}) copy-start(bf16[768,256]{1,0:T(8,128)(2,1)} %b_hbm.1) | copy-start | bytes 1179652
  1.7 0.9 %copy-start.1 = (f32[256,256]{1,0:T(8,128)S(1)}, f32[256,256]{1,0:T(8,128)}, u32[]{:S(2)}) copy-start(f32[256,256]{1,0:T(8,128)} %stored.1) | copy-start | bytes 786436
  2.6 0.9 %copy-start.2 = (f32[256,256]{1,0:T(8,128)S(1)}, f32[256,256]{1,0:T(8,128)}, u32[]{:S(2)}) copy-start(f32[256,256]{1,0:T(8,128)} %den.1) | copy-start | bytes 786436
  3.6 0.7 copy-start.3

commit v2 on v1

--- a/solution.py
+++ b/solution.py
@@ -12,19 +12,36 @@
 KB = 768
 HB = KB // 2
 NP = 6
-ORDER = [
-    (0, 0), (1, 0), (0, 1), (1, 1), (2, 0), (0, 2), (1, 2), (2, 1), (3, 0), (0, 3), (1, 3), (2, 2), (3, 1),
-    (0, 4), "B", (0, None), (1, 4), (2, 3), (3, 2), (1, None), (2, 4), (3, 3), (2, None), (3, 4), (3, None),
-]
+PACE = 0.6
+EXTRA = {(0, 1): "B1", (0, 2): "B2", (0, 3): "B3"}
+ORDER = []
+for _, _s, _t in sorted((s + PACE * t, s, t) for t in range(4) for s in range(5)):
+    ORDER += [EXTRA[_t, _s]] if (_t, _s) in EXTRA else []
+    ORDER.append((_t, _s))
+    if _s == 4:
+        ORDER += (["B4"] if _t == 0 else []) + [(_t, None)]
 
 
 def iota(shape, dim):
     return lax.broadcasted_iota(I32, shape, dim)
 
 
+def shr(a, n):
+    return lax.shift_right_logical(a, n)
+
+
+def first_row(block):
+    xx = jnp.bitwise_and(block, 3)
+    return jnp.bitwise_and(xx, 1) * 128 + shr(block, 2) * 32 + shr(xx, 1) * 16
+
+
+def block_of(row):
+    return jnp.bitwise_and(shr(row, 5), 3) * 4 + jnp.bitwise_and(shr(row, 4), 1) * 2 + shr(row, 7)
+
+
 def kernel(
-    stored, dest, mask, b_hbm, den, out,
-    t_ref, sib, merged, a_ref, b_ref, c_tx, c_rx, slots, w_ref,
+    stored_h, dest_h, mask_h, b_hbm, den_h, out,
+    stored, dest, mask, den, in_s, t_ref, sib, merged, a_ref, b_ref, c_tx, c_rx, slots, w_ref,
     sib_s, a1_s, a_s, a_r, b_s, b_r, bs_s, bs_r, bl_s, c_s, c_r, q_s, q_r,
 ):
     r, c = lax.axis_index("row"), lax.axis_index("col")
@@ -46,6 +63,12 @@
     def arrived(ref, sem):
         pltpu.make_async_copy(ref, ref, sem).wait()
 
+    ins = [
+        pltpu.make_async_copy(src, dst, in_s.at[i])
+        for i, (src, dst) in enumerate(((dest_h, dest), (mask_h, mask), (stored_h, stored), (den_h, den)))
+    ]
+    for cp in ins:
+        cp.start()
     bar = pltpu.get_barrier_semaphore()
 
     def hello(d):
@@ -67,25 +90,29 @@
 
     own_b = pltpu.make_async_copy(b_hbm, b_ref.at[k, pl.ds(x * KB, KB)], bl_s)
     own_b.start()
+    ins[0].wait()
     d = dest[...]
-    blk = lax.shift_right_logical(d, 8)
+    blk = shr(d, 8)
     low = jnp.bitwise_and(d, 255)
     oh = (iota((16, T), 0) == blk).astype(F32)
     before = (iota((T, T), 0) < iota((T, T), 1)).astype(F32).astype(BF)
     cum = jnp.dot(oh.astype(BF), before, preferred_element_type=F32)
     rank = jnp.sum(oh * cum, axis=0, keepdims=True)
-    pos = blk * 16 + rank.astype(I32)
+    pos = first_row(blk) + rank.astype(I32)
     perm = iota((T, T), 0) == pos
+    ins[1].wait()
     tm = mask[...].astype(F32).astype(BF)
-    spread = (lax.shift_right_logical(iota((T, 16), 0), 4) == iota((T, 16), 1)).astype(F32).astype(BF)
+    spread = (block_of(iota((T, 16), 0)) == iota((T, 16), 1)).astype(F32).astype(BF)
     wide = jnp.dot(spread, tm, preferred_element_type=F32)
     keep = jnp.sum(jnp.where(iota(wide.shape, 1) == c, wide, 0.0), axis=1, keepdims=True)
     permf = perm.astype(F32)
+    ins[2].wait()
     t_ref[...] = jnp.dot((permf * keep).astype(BF), stored[...].astype(BF), preferred_element_type=F32).astype(BF)
     low8 = jnp.broadcast_to(low, (8, T)).astype(F32).astype(BF)
     srow = lax.dot_general(low8, permf.astype(BF), (((1,), (1,)), ((), ())), preferred_element_type=F32)
     slots[r] = srow[:1]
-    half = (k * 8 + lax.shift_right_logical(iota((128, 16), 0), 4) == iota((128, 16), 1)).astype(F32).astype(BF)
+    row = iota((512, 16), 0)
+    half = (shr(row, 7) * 4 + jnp.bitwise_and(shr(row, 4), 1) * 2 + k == iota((512, 16), 1)).astype(F32).astype(BF)
     pick = (iota((48, 128), 0) == 12 * zl + iota((48, 128), 1)).astype(F32).astype(BF)
     tiles = jnp.dot(half, tm, preferred_element_type=F32).astype(BF)
     w_ref[...] = jnp.dot(tiles, pick, preferred_element_type=F32)
@@ -113,19 +140,20 @@
 
     j = zh * 8 + y
     tzl, tp = j // 6, j % 6
-    a1 = []
-    for h in range(NZH):
-        self_ = jnp.logical_and(tzl == zl, zh == h)
-        cp = remote(merged, a_ref.at[zl, tp], a1_s.at[h], a_r.at[zl, tp], dev(x, y, tzl, h, k))
-        a1.append((jnp.logical_not(self_), cp))
-
-        @pl.when(jnp.logical_not(self_))
-        def _():
-            cp.start()
-
-        @pl.when(self_)
-        def _():
-            pltpu.make_async_copy(merged, a_ref.at[zl, tp], a_r.at[zl, tp]).start()
+    def a1_self(h):
+        return jnp.logical_and(tzl == zl, zh == h)
+
+    for t in range(4):
+        for h in range(NZH):
+            src, dst = merged.at[pl.ds(t * 32, 32)], a_ref.at[t, tp, zl]
+
+            @pl.when(jnp.logical_not(a1_self(h)))
+            def _():
+                remote(src, dst, a1_s.at[h], a_r.at[t, tp], dev(x, y, tzl, h, k)).start()
+
+            @pl.when(a1_self(h))
+            def _():
+                pltpu.make_async_copy(src, dst, a_r.at[t, tp]).start()
 
     def slot_cp(i):
         o = (r + i) % 16
@@ -150,10 +178,6 @@
     relay1 = remote(bslot(k, xb, 1), bslot(k, xb, 1), b_s.at[5], b_r.at[xb, 1], xl)
     relay1.start()
     b_out += [relay0, relay1]
-    to_sibling(b_hbm.at[top], x, 0)
-    to_sibling(b_hbm.at[bot], x, 1)
-    to_sibling(bslot(k, xa, 0), xa, 0)
-    to_sibling(bslot(k, xb, 1), xb, 1)
 
     u = (y + 2 * zl) % 8
 
@@ -186,10 +210,9 @@
                         else:
                             a_cp(q, p, w).start()
 
-    def c_send(q, i, act):
-        o, n = k * 8 + i % 8, i // 8
-        src = c_tx.at[q * 16 + i]
-        dst = c_rx.at[zl, q * 4 + x]
+    def c_send(t, n, xh):
+        o = t * 4 + xh * 2 + k
+        src, dst = c_tx.at[t * 4 + n * 2 + xh], c_rx.at[zl, x]
         self_ = jnp.logical_and(o == r, n == k)
 
         @pl.when(jnp.logical_not(self_))
@@ -200,27 +223,36 @@
         def _():
             pltpu.make_async_copy(src, dst, c_r).start()
 
-    def product(q):
-        w = w_ref[...]
+    def product(t):
+        w = w_ref[t * 128 : (t + 1) * 128]
         for n in range(2):
             acc = jnp.zeros((128, T), F32)
             for p in range(NP):
-                a = a_ref[q, p]
+                a = a_ref[t, p].reshape(128, T)
                 for e in range(2):
                     keep_ = w[:, 2 * p + e : 2 * p + e + 1] > 0.5
                     lhs = jnp.where(keep_, a.astype(F32), 0.0).astype(BF)
                     acc = acc + jnp.dot(lhs, b_ref[n, (2 * p + e) * T : (2 * p + e + 1) * T], preferred_element_type=F32)
-            c_tx[q * 16 + n * 8 : q * 16 + n * 8 + 8] = acc.astype(BF).reshape(8, 16, T)
-
-        @pl.loop(0, 16)
-        def _(i):
-            c_send(q, i, None)
+            acc = acc.astype(BF).reshape(4, 2, 16, T)
+            for xh in range(2):
+                c_tx[t * 4 + n * 2 + xh] = acc[:, xh]
+                c_send(t, n, xh)
 
     for step in ORDER:
-        if step == "B":
-            for xx, h in ((xa, 1), (xb, 0), (xc, 0), (xc, 1)):
+        if step == "B1":
+            to_sibling(b_hbm.at[top], x, 0)
+            to_sibling(b_hbm.at[bot], x, 1)
+            to_sibling(bslot(k, xa, 0), xa, 0)
+            to_sibling(bslot(k, xb, 1), xb, 1)
+        elif step == "B2":
+            for xx, h in ((xa, 1), (xb, 0)):
                 arrived(bslot(k, xx, h), b_r.at[xx, h])
                 to_sibling(bslot(k, xx, h), xx, h)
+        elif step == "B3":
+            for xx, h in ((xc, 0), (xc, 1)):
+                arrived(bslot(k, xx, h), b_r.at[xx, h])
+                to_sibling(bslot(k, xx, h), xx, h)
+        elif step == "B4":
             own_b.wait()
             for xx in range(4):
                 for h in range(2):
@@ -231,37 +263,39 @@
             ring(*step)
 
     to_sib.wait_send()
-    for ok, cp in a1:
-
-        @pl.when(ok)
+    for h in range(NZH):
+
+        @pl.when(jnp.logical_not(a1_self(h)))
         def _():
-            cp.wait_send()
+            arrived(merged, a1_s.at[h])
 
     for cp in b_out + b_sib:
         cp.wait_send()
     for step in ORDER:
-        if step != "B" and step[1] is not None and step[1] < 4:
+        if step[0] != "B" and step[1] is not None and step[1] < 4:
             ring(*step, waits=True)
     arrived(slots.at[pl.ds(0, 15)], q_s)
     arrived(slots.at[pl.ds(0, 15)], q_r)
 
-    sel = (iota((T, T), 0) == r * 16 + jnp.bitwise_and(iota((T, T), 1), 15)).astype(F32).astype(BF)
+    sel = (iota((T, T), 0) == first_row(r) + jnp.bitwise_and(iota((T, T), 1), 15)).astype(F32).astype(BF)
     g = jnp.dot(slots[...].reshape(16, T).astype(BF), sel, preferred_element_type=F32)
-    own = lax.shift_right_logical(iota((16, T), 1), 4) == iota((16, T), 0)
+    lane = iota((16, T), 1)
+    own = jnp.bitwise_and(shr(lane, 4), 3) * 4 + shr(lane, 6) == iota((16, T), 0)
     at = jnp.sum(jnp.where(own, g, 0.0), axis=0, keepdims=True).astype(I32)
     place = (iota((T, T), 0) == at).astype(F32).astype(BF)
 
+    ins[3].wait()
     arrived(c_rx, c_r)
     total = jnp.zeros((T, T), F32)
     for g in range(NZL):
         total = total + jnp.dot(place, c_rx[g].reshape(T, T), preferred_element_type=F32)
     out[...] = total / den[...]
 
-    has_own = (r // 8) == k
+    has_own = x % 2 == k
 
     @pl.when(has_own)
     def _():
-        arrived(c_tx.at[pl.ds(0, 60)], c_s)
+        arrived(c_tx.at[pl.ds(0, 15)], c_s)
 
     @pl.when(jnp.logical_not(has_own))
     def _():
@@ -274,18 +308,23 @@
     return pl.pallas_call(
         kernel,
         out_shape=jax.ShapeDtypeStruct((T, T), F32),
-        in_specs=[vm, vm, vm, pl.BlockSpec(memory_space=pl.ANY), vm],
+        in_specs=[pl.BlockSpec(memory_space=pltpu.HBM)] * 5,
         out_specs=vm,
         scratch_shapes=[
+            pltpu.VMEM((T, T), F32),
+            pltpu.VMEM((1, T), I32),
+            pltpu.VMEM((16, 48), I32),
+            pltpu.VMEM((T, T), F32),
+            dma((4,)),
             pltpu.VMEM((T, T), BF),
             pltpu.VMEM((128, T), BF),
             pltpu.VMEM((128, T), BF),
-            pltpu.VMEM((4, NP, 128, T), BF),
+            pltpu.VMEM((4, NP, 4, 32, T), BF),
             pltpu.VMEM((2, 4 * KB, T), BF),
-            pltpu.VMEM((64, 16, T), BF),
-            pltpu.VMEM((4, 16, 16, T), BF),
+            pltpu.VMEM((16, 4, 16, T), BF),
+            pltpu.VMEM((4, 4, 4, 16, T), BF),
             pltpu.VMEM((16, 1, T), F32),
-            pltpu.VMEM((128, 128), F32),
+            pltpu.VMEM((512, 128), F32),
             dma((2,)),
             dma((3,)),
             dma((4, NP, 2)),
@@ -301,7 +340,7 @@
             dma,
         ],
         compiler_params=pltpu.CompilerParams(
-            collective_id=0, has_side_effects=True, vmem_limit_bytes=40 << 20
+            collective_id=0, has_side_effects=True, vmem_limit_bytes=62 << 20
         ),
         name="ladder",
     )(stored, destination.reshape(1, T), tile_mask, integrals, denominators)

time: 72.5 us -> 60.8 us (0.84)
  the two profiles are of different devices: /device:TPU:1 before, /device:TPU:65 now
where the time goes in v2:
time: 60.8 us; the launch traced here: 60.6 us
  Pallas kernels  58.9 us (97%)
  local copies, waits for them, and re-layouts  1.67 us (3%)
    pallas_call x1, Pallas kernels, local(): pl.pallas_call(kernel, out_shape=jax.ShapeDtypeStruct((T, T), F32), in_sp...  58.9 us
    unnamed x1, local copies, waits for them, and re-layouts  1.67 us

profile of v2, /device:TPU:65, one launch (start us, length us, event | category | flops | bytes accessed | tf_op | source)
XLA Modules:
  0.0 60.6 jit_solution(7507438561834214837)
XLA Ops:
  0.0 58.9 %ladder.1 = f32[256,256]{1,0:T(8,128)} custom-call(f32[256,256]{1,0:T(8,128)} %stored_h.1, s32[1,256]{1,0:T(1,128)} %bitcast.1, s32[16,48]{1,0:T(8,128)} %mask_h.1, bf16[768,256]{1,0:T(8,128)(2,1)} %b_hbm.1, f32[256,256]{1,0:T(8,128)} %den_h.1), custom_call_target="tpu_custom_call" | custom-call | tf_op jit(solution)/shard_map/ladder/pallas_call | solution.py:308
  58.9 1.7 %copy.7 = f32[256,256]{1,0:T(8,128)} copy(f32[256,256]{1,0:T(8,128)} %ladder.1) | data formatting | bytes 524288

commit v3 on v2

--- a/solution.py
+++ b/solution.py
@@ -12,12 +12,14 @@
 KB = 768
 HB = KB // 2
 NP = 6
-PACE = 0.6
+PACE = 0.7
 EXTRA = {(0, 1): "B1", (0, 2): "B2", (0, 3): "B3"}
+LATER = {(0, 0): ["A2"], (1, 0): ["A3"]}
 ORDER = []
 for _, _s, _t in sorted((s + PACE * t, s, t) for t in range(4) for s in range(5)):
     ORDER += [EXTRA[_t, _s]] if (_t, _s) in EXTRA else []
     ORDER.append((_t, _s))
+    ORDER += LATER.get((_t, _s), [])
     if _s == 4:
         ORDER += (["B4"] if _t == 0 else []) + [(_t, None)]
 
@@ -32,16 +34,21 @@
 
 def first_row(block):
     xx = jnp.bitwise_and(block, 3)
-    return jnp.bitwise_and(xx, 1) * 128 + shr(block, 2) * 32 + shr(xx, 1) * 16
+    chunk = jnp.bitwise_xor(shr(block, 2), shr(xx, 1))
+    return jnp.bitwise_and(xx, 1) * 128 + chunk * 32 + shr(xx, 1) * 16
+
+
+def target(chunk, xh, core):
+    return jnp.bitwise_xor(chunk, xh) * 4 + xh * 2 + core
 
 
 def block_of(row):
-    return jnp.bitwise_and(shr(row, 5), 3) * 4 + jnp.bitwise_and(shr(row, 4), 1) * 2 + shr(row, 7)
+    return target(jnp.bitwise_and(shr(row, 5), 3), jnp.bitwise_and(shr(row, 4), 1), shr(row, 7))
 
 
 def kernel(
     stored_h, dest_h, mask_h, b_hbm, den_h, out,
-    stored, dest, mask, den, in_s, t_ref, sib, merged, a_ref, b_ref, c_tx, c_rx, slots, w_ref,
+    stored, dest, mask, den, in_s, t_ref, sib, merged, a_ref, b_ref, c_tx, c_rx, slots, slot_out, w_ref,
     sib_s, a1_s, a_s, a_r, b_s, b_r, bs_s, bs_r, bl_s, c_s, c_r, q_s, q_r,
 ):
     r, c = lax.axis_index("row"), lax.axis_index("col")
@@ -74,19 +81,30 @@
     def hello(d):
         pl.semaphore_signal(bar, inc=1, device_id=d, device_id_type=MESH)
 
-    @pl.loop(0, 8)
+    j, u = zh * 8 + y, (y + 2 * zl) % 8
+    tzl, tp = j // NP, j % NP
+    for d in (sibling, xr, xl, yr, yl):
+        hello(d)
+
+    src_zh = (NP * zl + u) // 8
+
+    @pl.when(u < NP)
+    def _():
+        for q in range(NZL):
+
+            @pl.when(jnp.logical_not(jnp.logical_and(q == zl, src_zh == zh)))
+            def _():
+                hello(dev(x, y, q, src_zh, k))
+
+    giver = x % 2
+
+    @pl.loop(0, 16)
     def _(i):
-        hello(dev(x, y, i % 4, (zh + 1 + i // 4) % 3, k))
-
-    me = r * 2 + k
-
-    @pl.loop(1, 32)
-    def _(i):
-        o = (me + i) % 32
-        hello((o // 2, c - k + o % 2))
-
-    hello(yr)
-    hello(yl)
+        @pl.when(jnp.logical_or(i != r, giver != k))
+        def _():
+            hello((i, c - k + giver))
+
+    greeted = 5 + NZH - (tzl == zl).astype(I32) + 16 - (giver == k).astype(I32)
 
     own_b = pltpu.make_async_copy(b_hbm, b_ref.at[k, pl.ds(x * KB, KB)], bl_s)
     own_b.start()
@@ -105,19 +123,11 @@
     spread = (block_of(iota((T, 16), 0)) == iota((T, 16), 1)).astype(F32).astype(BF)
     wide = jnp.dot(spread, tm, preferred_element_type=F32)
     keep = jnp.sum(jnp.where(iota(wide.shape, 1) == c, wide, 0.0), axis=1, keepdims=True)
-    permf = perm.astype(F32)
+    sorting = (perm.astype(F32) * keep).astype(BF)
     ins[2].wait()
-    t_ref[...] = jnp.dot((permf * keep).astype(BF), stored[...].astype(BF), preferred_element_type=F32).astype(BF)
-    low8 = jnp.broadcast_to(low, (8, T)).astype(F32).astype(BF)
-    srow = lax.dot_general(low8, permf.astype(BF), (((1,), (1,)), ((), ())), preferred_element_type=F32)
-    slots[r] = srow[:1]
-    row = iota((512, 16), 0)
-    half = (shr(row, 7) * 4 + jnp.bitwise_and(shr(row, 4), 1) * 2 + k == iota((512, 16), 1)).astype(F32).astype(BF)
-    pick = (iota((48, 128), 0) == 12 * zl + iota((48, 128), 1)).astype(F32).astype(BF)
-    tiles = jnp.dot(half, tm, preferred_element_type=F32).astype(BF)
-    w_ref[...] = jnp.dot(tiles, pick, preferred_element_type=F32)
-
-    pl.semaphore_wait(bar, 41)
+    t_ref[...] = jnp.dot(sorting, stored[...].astype(BF), preferred_element_type=F32).astype(BF)
+
+    pl.semaphore_wait(bar, greeted)
 
     away, mine = pl.ds((1 - k) * 128, 128), pl.ds(k * 128, 128)
     to_sib = remote(t_ref.at[away], sib, sib_s.at[0], sib_s.at[1], sibling)
@@ -138,12 +148,10 @@
     to_sib.wait_recv()
     merged[...] = t_ref[mine] + sib[...]
 
-    j = zh * 8 + y
-    tzl, tp = j // 6, j % 6
     def a1_self(h):
         return jnp.logical_and(tzl == zl, zh == h)
 
-    for t in range(4):
+    def a1_send(t):
         for h in range(NZH):
             src, dst = merged.at[pl.ds(t * 32, 32)], a_ref.at[t, tp, zl]
 
@@ -155,13 +163,30 @@
             def _():
                 pltpu.make_async_copy(src, dst, a_r.at[t, tp]).start()
 
-    def slot_cp(i):
-        o = (r + i) % 16
-        return remote(slots.at[r], slots.at[r], q_s, q_r, (o, c))
-
-    @pl.loop(1, 16)
+    for t in range(2):
+        a1_send(t)
+
+    low8 = jnp.broadcast_to(low, (8, T)).astype(F32).astype(BF)
+    srow = lax.dot_general(low8, perm.astype(F32).astype(BF), (((1,), (1,)), ((), ())), preferred_element_type=F32)
+    slot_out[0] = srow[:1]
+    row = iota((512, 16), 0)
+    half = (target(shr(row, 7), jnp.bitwise_and(shr(row, 4), 1), k) == iota((512, 16), 1)).astype(F32).astype(BF)
+    pick = (iota((48, 128), 0) == 12 * zl + iota((48, 128), 1)).astype(F32).astype(BF)
+    tiles = jnp.dot(half, tm, preferred_element_type=F32).astype(BF)
+    w_ref[...] = jnp.dot(tiles, pick, preferred_element_type=F32)
+
+    @pl.loop(0, 16)
     def _(i):
-        slot_cp(i).start()
+        o, n = i // 4 * 4 + i // 2 % 2 * 2 + k, i % 2
+        self_ = jnp.logical_and(o == r, n == k)
+
+        @pl.when(jnp.logical_not(self_))
+        def _():
+            remote(slot_out.at[0], slots.at[r], q_s, q_r, (o, c - k + n)).start()
+
+        @pl.when(self_)
+        def _():
+            pltpu.make_async_copy(slot_out.at[0], slots.at[r], q_r).start()
 
     xa, xb, xc = (x + 3) % 4, (x + 1) % 4, (x + 2) % 4
     b_sib = []
@@ -179,18 +204,19 @@
     relay1.start()
     b_out += [relay0, relay1]
 
-    u = (y + 2 * zl) % 8
-
-    def a_cp(q, p, way):
-        return remote(a_ref.at[q, p], a_ref.at[q, p], a_s.at[q, p, way], a_r.at[q, p], (yr, yl)[way])
+    def part(i, p):
+        return a_ref.at[i, p]
+
+    def a_cp(i, p, way):
+        return remote(part(i, p), part(i, p), a_s.at[i, p, way], a_r.at[i, p], (yr, yl)[way])
 
     def reach(p, way):
         far = jnp.where(p >= 3, 1, 0)
         return 3 + far if way == 0 else 4 - far
 
-    def ring(q, s, waits=False):
+    def ring(i, s, waits=False):
         for way in ((0, 1) if s else (0,)):
-            p = (u - s + 8 * way + 8 - 8 * way) % 8 if way == 0 else (u + s) % 8
+            p = jnp.bitwise_and(u + (8 - s if way == 0 else s), 7)
             valid = p < NP
             if s:
                 valid = jnp.logical_and(valid, s <= reach(p, way))
@@ -198,7 +224,7 @@
             @pl.when(valid)
             def _():
                 if not waits:
-                    arrived(a_ref.at[q, p], a_r.at[q, p])
+                    arrived(part(i, p), a_r.at[i, p])
                 for w in ((way,) if s else (0, 1)):
                     if s >= 4:
                         continue
@@ -206,12 +232,12 @@
                     @pl.when(s < reach(p, w))
                     def _():
                         if waits:
-                            a_cp(q, p, w).wait_send()
+                            a_cp(i, p, w).wait_send()
                         else:
-                            a_cp(q, p, w).start()
+                            a_cp(i, p, w).start()
 
     def c_send(t, n, xh):
-        o = t * 4 + xh * 2 + k
+        o = target(t, xh, k)
         src, dst = c_tx.at[t * 4 + n * 2 + xh], c_rx.at[zl, x]
         self_ = jnp.logical_and(o == r, n == k)
 
@@ -239,7 +265,9 @@
                 c_send(t, n, xh)
 
     for step in ORDER:
-        if step == "B1":
+        if step[0] == "A":
+            a1_send(int(step[1]))
+        elif step == "B1":
             to_sibling(b_hbm.at[top], x, 0)
             to_sibling(b_hbm.at[bot], x, 1)
             to_sibling(bslot(k, xa, 0), xa, 0)
@@ -272,10 +300,9 @@
     for cp in b_out + b_sib:
         cp.wait_send()
     for step in ORDER:
-        if step[0] != "B" and step[1] is not None and step[1] < 4:
+        if step[0] not in ("A", "B") and step[1] is not None and step[1] < 4:
             ring(*step, waits=True)
-    arrived(slots.at[pl.ds(0, 15)], q_s)
-    arrived(slots.at[pl.ds(0, 15)], q_r)
+    arrived(slots, q_r)
 
     sel = (iota((T, T), 0) == first_row(r) + jnp.bitwise_and(iota((T, T), 1), 15)).astype(F32).astype(BF)
     g = jnp.dot(slots[...].reshape(16, T).astype(BF), sel, preferred_element_type=F32)
@@ -296,10 +323,12 @@
     @pl.when(has_own)
     def _():
         arrived(c_tx.at[pl.ds(0, 15)], c_s)
+        arrived(slots.at[pl.ds(0, 15)], q_s)
 
     @pl.when(jnp.logical_not(has_own))
     def _():
         arrived(c_tx, c_s)
+        arrived(slots, q_s)
 
 
 def local(stored, destination, tile_mask, integrals, denominators):
@@ -324,6 +353,7 @@
             pltpu.VMEM((16, 4, 16, T), BF),
             pltpu.VMEM((4, 4, 4, 16, T), BF),
             pltpu.VMEM((16, 1, T), F32),
+            pltpu.VMEM((1, 1, T), F32),
             pltpu.VMEM((512, 128), F32),
             dma((2,)),
             dma((3,)),

time: 60.8 us -> 59.5 us (0.979)
  the two profiles are of different devices: /device:TPU:65 before, /device:TPU:193 now
where the time goes in v3:
time: 59.5 us; the launch traced here: 59.3 us
  Pallas kernels  57.6 us (97%)
  local copies, waits for them, and re-layouts  1.67 us (3%)
    pallas_call x1, Pallas kernels, local(): pl.pallas_call(kernel, out_shape=jax.ShapeDtypeStruct((T, T), F32), in_sp...  57.6 us
    unnamed x1, local copies, waits for them, and re-layouts  1.67 us

profile of v3, /device:TPU:193, one launch (start us, length us, event | category | flops | bytes accessed | tf_op | source)
XLA Modules:
  0.0 59.3 jit_solution(15265339113783620564)
XLA Ops:
  0.0 57.6 %ladder.1 = f32[256,256]{1,0:T(8,128)} custom-call(f32[256,256]{1,0:T(8,128)} %stored_h.1, s32[1,256]{1,0:T(1,128)} %bitcast.1, s32[16,48]{1,0:T(8,128)} %mask_h.1, bf16[768,256]{1,0:T(8,128)(2,1)} %b_hbm.1, f32[256,256]{1,0:T(8,128)} %den_h.1), custom_call_target="tpu_custom_call" | custom-call | tf_op jit(solution)/shard_map/ladder/pallas_call | solution.py:337
  57.6 1.7 %copy.7 = f32[256,256]{1,0:T(8,128)} copy(f32[256,256]{1,0:T(8,128)} %ladder.1) | data formatting | bytes 524288
